TPU v7x, 32 devices: a whole 2x2x4 slice. The times are simulated.
32 devices in a mesh: tm: 4 (over x, core), cols: 8 (over z, y).
Axes of the slice: x: 2, y: 2, z: 4, core: 2. Of those that a mesh axis runs over, the one named last changes fastest.
Arguments:
- inv_diag: bfloat16 [4, 2048, 2048], P('tm', 'cols'), as said below
- sub_diag: bfloat16 [4, 2048, 2048], P('tm', 'cols'), may hold values from -0.09375 to 0.09375
- rhs: bfloat16 [4, 2048, 4096], P('tm', None, 'cols'), may hold values from -6 to 6
- carry_in: bfloat16 [2048, 4096], P(None, 'cols'), may hold values from -6 to 6
Outputs:
- solved: float32 [4, 2048, 4096], P('tm', None, 'cols')
Inputs may be any that keep to these rules, and one draw needn't show every extreme that they name: Each block of inv_diag is lower triangular with diagonal entries between 0.5 and 1.5.
All inputs are finite; a program needn't handle non-finite values.
Results may differ from a plain program's by a relative error of at most 0.007.
Values may be sent and summed in bfloat16 or wider, within the bound.
A program may use at most 128 MiB of HBM per device.

v0:
```python
import jax
import jax.numpy as jnp
from jax import lax
from jax.sharding import PartitionSpec as P


def shifted(shard, axis, by):
    devices = lax.axis_size(axis)
    pairs = [(i, i + by) for i in range(devices) if 0 <= i + by < devices]
    return lax.ppermute(shard, axis, pairs)


def shards(inv_diag, sub_diag, rhs, carry_in):
    sections = lax.axis_size("tm")
    section = lax.axis_index("tm")
    sample_cols = rhs.shape[2]
    inv_full, sub_full = (
        lax.all_gather(inv_diag, "cols", axis=1, tiled=True),
        lax.all_gather(sub_diag, "cols", axis=1, tiled=True),
    )
    batch_count = 1
    piece_cols = sample_cols // batch_count
    solved = jnp.zeros(rhs.shape, jnp.float32)
    incoming = jnp.zeros((rhs.shape[1], piece_cols), jnp.bfloat16)
    timesteps = sections + batch_count - 1
    for timestep in range(timesteps):
        micro_batch = timestep - section
        active = jnp.logical_and(micro_batch >= 0, micro_batch < batch_count)
        which_batch = jnp.clip(micro_batch, 0, batch_count - 1)
        first_col = which_batch * piece_cols

        def compute_batch(operands):
            solved_now, incoming_now = operands
            previous = jnp.where(section == 0, carry_in, incoming_now)
            source = rhs[0]
            coupled = jnp.dot(sub_full[0], previous, preferred_element_type=jnp.float32)
            update = (source.astype(jnp.float32) - coupled).astype(jnp.bfloat16)
            result = jnp.dot(inv_full[0], update, preferred_element_type=jnp.float32)
            columns = [result]
            previous = result.astype(jnp.bfloat16)
            stacked = jnp.stack(columns)
            return (lax.dynamic_update_slice_in_dim(solved_now, stacked, first_col, 2), previous)

        def skip_batch(operands):
            return (operands[0], jnp.zeros_like(operands[1]))

        solved, outgoing = lax.cond(active, compute_batch, skip_batch, (solved, incoming))
        if timestep + 1 < timesteps:
            incoming = shifted(outgoing, "tm", 1)
    return solved


def solution(mesh):
    in_specs = (
        P("tm", "cols", None),
        P("tm", "cols", None),
        P("tm", None, "cols"),
        P(None, "cols"),
    )
    out_specs = P("tm", None, "cols")
    return jax.shard_map(shards, mesh=mesh, in_specs=in_specs, out_specs=out_specs, check_vma=False)
```

profile of v0, /device:TPU:1, one launch (start us, length us, event | category | flops | bytes accessed | tf_op | source)
XLA Modules:
  0.0 403.1 jit_solution(12865336972657975961)
XLA Ops:
  6.5 0.0 all-gather.3.cloned.1.call-start
  6.5 0.7 all-gather.3.cloned.1.call-update
  7.3 0.0 all-gather.5.cloned.1.call-start
  7.3 0.7 all-gather.5.cloned.1.call-update
  8.0 128.1 %all-gather.3.cloned.1.call-done = bf16[1,2048,2048]{2,1,0:T(8,128)(2,1)} async-done(((bf16[1,256,2048]{2,1,0:T(8,128)(2,1)}), bf16[1,2048,2048]{2,1,0:T(8,128)(2,1)}) %all-gather.3.cloned.1.call-update) | async-done | bytes 8388624 | tf_op jit(solution)/shard_map/all_gather | solution.py:19
  136.1 125.3 %all-gather.5.cloned.1.call-done = bf16[1,2048,2048]{2,1,0:T(8,128)(2,1)} async-done(((bf16[1,256,2048]{2,1,0:T(8,128)(2,1)}), bf16[1,2048,2048]{2,1,0:T(8,128)(2,1)}) %all-gather.5.cloned.1.call-update) | async-done | bytes 8388624 | tf_op jit(solution)/shard_map/all_gather | solution.py:18
  261.4 2.7 conditional.4
  261.4 2.5 broadcast_in_dim.2
  263.9 0.2 broadcast.9
  264.1 2.5 copy.7
  266.6 4.0 %collective-permute-start = (bf16[2048,512]{1,0:T(8,128)(2,1)}, bf16[2048,512]{1,0:T(8,128)(2,1)S(1)}, u32[]{:S(2)}, u32[]{:S(2)}) collective-permute-start(bf16[2048,512]{1,0:T(8,128)(2,1)} %copy.7), channel_id=1, source_target_pairs={{0,8},{8,16},{16,24},{1,9},{9,17},{17,25},{2,10},{10,18},{18,26},{... | collective-permute-start | bytes 6291464 | tf_op jit(solution)/shard_map/ppermute | solution.py:10
  270.7 23.3 %collective-permute-done = bf16[2048,512]{1,0:T(8,128)(2,1)S(1)} collective-permute-done((bf16[2048,512]{1,0:T(8,128)(2,1)}, bf16[2048,512]{1,0:T(8,128)(2,1)S(1)}, u32[]{:S(2)}, u32[]{:S(2)}) %collective-permute-start) | collective-permute-done | bytes 2097184 | tf_op jit(solution)/shard_map/ppermute | solution.py:10
  293.9 19.3 %conditional.5 = (f32[1,2048,512]{1,2,0:T(8,128)}, bf16[2048,512]{0,1:T(8,128)(2,1)S(1)}) conditional(s32[]{:T(128)} %convert_element_type.70, f32[1,2048,512]{1,2,0:T(8,128)} %get-tuple-element.140, (bf16[1,2048,512]{2,1,0:T(8,128)(2,1)}, s32[]{:T(128)}, bf16[2048,512]{1,0:T(8,128)(2,1)}, bf16[2048,512]{1,0:T(8,128)(2,1)S(1)}, ...), branch_computations={%region_2.3_spmd, %region_3.4_spmd} | conditional | flops 8595177472 | bytes 37748788 | solution.py:47
  294.1 0.0 copy-start.1
  294.1 1.3 copy-done.1
  295.4 17.8 %bitcast_convert_fusion.1 = (bf16[2048,512]{0,1:T(8,128)(2,1)S(1)}, f32[512,2048]{1,0:T(8,128)}) fusion(bf16[1,2048,2048]{2,1,0:T(8,128)(2,1)} %get-tuple-element.121, bf16[1,2048,2048]{2,1,0:T(8,128)(2,1)} %get-tuple-element.120, bf16[1,2048,512]{2,1,0:T(8,128)(2,1)} %get-tuple-element.116, bf16[2048,512]{1,0:T(8,128)(2,1)} %get-tuple-element.118, ...), kind=kOutput, calls=%fused_computation.18 | convolution fusion | flops 8595177472 | bytes 29360128 | tf_op jit(solution)/shard_map/cond/branch_1_fun/dot_general | solution.py:38
  313.2 2.5 copy.8
  315.7 1.9 collective-permute-start.1
  317.6 23.3 %collective-permute-done.1 = bf16[2048,512]{1,0:T(8,128)(2,1)S(1)} collective-permute-done((bf16[2048,512]{1,0:T(8,128)(2,1)}, bf16[2048,512]{1,0:T(8,128)(2,1)S(1)}, u32[]{:S(2)}, u32[]{:S(2)}) %collective-permute-start.1) | collective-permute-done | bytes 2097184 | tf_op jit(solution)/shard_map/ppermute | solution.py:10
  340.9 0.5 conditional.6
  340.9 0.2 broadcast.12
  341.4 2.5 copy.9
  343.9 23.1 %collective-permute-start.2 = (bf16[2048,512]{1,0:T(8,128)(2,1)}, bf16[2048,512]{1,0:T(8,128)(2,1)S(1)}, u32[]{:S(2)}, u32[]{:S(2)}) collective-permute-start(bf16[2048,512]{1,0:T(8,128)(2,1)} %copy.9), channel_id=1, source_target_pairs={{0,8},{8,16},{16,24},{1,9},{9,17},{17,25},{2,10},{10,18},{18,26},{... | collective-permute-start | bytes 6291464 | tf_op jit(solution)/shard_map/ppermute | solution.py:10
  367.0 23.3 %collective-permute-done.2 = bf16[2048,512]{1,0:T(8,128)(2,1)S(1)} collective-permute-done((bf16[2048,512]{1,0:T(8,128)(2,1)}, bf16[2048,512]{1,0:T(8,128)(2,1)S(1)}, u32[]{:S(2)}, u32[]{:S(2)}) %collective-permute-start.2) | collective-permute-done | bytes 2097184 | tf_op jit(solution)/shard_map/ppermute | solution.py:10
  390.2 0.2 conditional.7
  390.5 5.3 %copy.10 = f32[1,2048,512]{2,1,0:T(8,128)} copy(f32[1,2048,512]{1,2,0:T(8,128)} %get-tuple-element.146) | data formatting | bytes 8388608
Async XLA Ops:
  6.5 129.6 %all-gather.3.cloned.1.call-start = ((), (), s32[]{:S(2)}) async-start(), calls=%async_computation | async-start | bytes 9437184 | tf_op jit(solution)/shard_map/all_gather | solution.py:19
  7.3 254.1 %all-gather.5.cloned.1.call-start = ((), (), s32[]{:S(2)}) async-start(), calls=%async_computation.1 | async-start | bytes 9437184 | tf_op jit(solution)/shard_map/all_gather | solution.py:18
  266.6 27.3 %collective-permute-start = (bf16[2048,512]{1,0:T(8,128)(2,1)}, bf16[2048,512]{1,0:T(8,128)(2,1)S(1)}, u32[]{:S(2)}, u32[]{:S(2)}) collective-permute-start(bf16[2048,512]{1,0:T(8,128)(2,1)} %copy.7), channel_id=1, source_target_pairs={{0,8},{8,16},{16,24},{1,9},{9,17},{17,25},{2,10},{10,18},{18,26},{... | collective-permute-start | bytes 6291464 | tf_op jit(solution)/shard_map/ppermute | solution.py:10
  294.1 1.3 copy-start.1
  315.7 25.2 %collective-permute-start.1 = (bf16[2048,512]{1,0:T(8,128)(2,1)}, bf16[2048,512]{1,0:T(8,128)(2,1)S(1)}, u32[]{:S(2)}, u32[]{:S(2)}) collective-permute-start(bf16[2048,512]{1,0:T(8,128)(2,1)} %copy.8), channel_id=1, source_target_pairs={{0,8},{8,16},{16,24},{1,9},{9,17},{17,25},{2,10},{10,18},{18,26},{... | collective-permute-start | bytes 6291464 | tf_op jit(solution)/shard_map/ppermute | solution.py:10
  343.9 46.4 %collective-permute-start.2 = (bf16[2048,512]{1,0:T(8,128)(2,1)}, bf16[2048,512]{1,0:T(8,128)(2,1)S(1)}, u32[]{:S(2)}, u32[]{:S(2)}) collective-permute-start(bf16[2048,512]{1,0:T(8,128)(2,1)} %copy.9), channel_id=1, source_target_pairs={{0,8},{8,16},{16,24},{1,9},{9,17},{17,25},{2,10},{10,18},{18,26},{... | collective-permute-start | bytes 6291464 | tf_op jit(solution)/shard_map/ppermute | solution.py:10
Sparse Core Ops, SparseCore 0:
  9.5 126.5 all-gather.2
  138.3 123.1 all-gather.4
where the time goes:
time: 410 us; the launch traced here: 403 us
  waiting for transfers between devices  325 us (79%)
  starting transfers between devices  29.1 us (7%)
  matrix products  17.8 us (4%)
  local copies, waits for them, and re-layouts  17.1 us (4%)
  between operations  13.9 us (3%)
    all_gather x1, waiting for transfers between devices, shards(): lax.all_gather(sub_diag, 'cols', axis=1, tiled=True)  128 us
    all_gather x1, waiting for transfers between devices, shards(): lax.all_gather(inv_diag, 'cols', axis=1, tiled=True)  125 us
    ppermute x3, waiting for transfers between devices, shifted(): return lax.ppermute(shard, axis, pairs)  69.8 us
    ppermute x3, starting transfers between devices, shifted(): return lax.ppermute(shard, axis, pairs)  29 us
    dot_general x1, matrix products, compute_batch(): result = jnp.dot(inv_full[0], update, preferred_element_type=jnp.float32)  17.8 us
  transfers between devices with their start and end apart: 5, of which 5 were waited for; matrix products, arithmetic and copies ran while one was open for 0% of the time, Pallas kernels for 0%

commit v1 on v0

v1 whole, which is shorter than its diff:
```python
import functools

import jax
import jax.numpy as jnp
from jax import lax
from jax.experimental import pallas as pl
from jax.experimental.pallas import tpu as pltpu
from jax.sharding import PartitionSpec as P

MESH = pl.DeviceIdType.MESH
WIDE = 512
BATCH = 256
UP, DOWN, ACROSS = 0, 1, 2


def kernel(sections, lines, inv_ref, sub_ref, rhs_ref, carry_ref, out_ref,
           factors, rhs, prior, update, solved, rounded,
           own_sem, load_sem, store_sem, send_sem, recv_sem, prior_send, prior_recv):
    section = lax.axis_index("tm")
    col = lax.axis_index("cols")
    z, y = col // 2, lax.rem(col, 2)
    rows = inv_ref.shape[1]
    order = inv_ref.shape[2]
    pieces = order // WIDE
    batches = rhs_ref.shape[2] // BATCH

    own_rows = pl.ds(pl.multiple_of(col * rows, rows), rows)
    own = [
        pltpu.make_async_copy(sub_ref.at[0], factors.at[0, own_rows, :], own_sem.at[0]),
        pltpu.make_async_copy(inv_ref.at[0], factors.at[1, own_rows, :], own_sem.at[1]),
    ]
    for copy in own:
        copy.start()
    loads = [pltpu.make_async_copy(rhs_ref.at[0], rhs, load_sem.at[0])]
    carries = [
        pltpu.make_async_copy(carry_ref.at[:, pl.ds(b * BATCH, BATCH)], prior.at[b], load_sem.at[1 + b])
        for b in range(batches)
    ]

    barrier = pltpu.get_barrier_semaphore()

    def greet(cond, device):
        @pl.when(cond)
        def _():
            pl.semaphore_signal(barrier, inc=1, device_id=device, device_id_type=MESH)

    greet(z > 0, {"cols": col - 2})
    greet(z < lines - 1, {"cols": col + 2})
    pl.semaphore_signal(barrier, inc=1, device_id={"cols": 2 * z + 1 - y}, device_id_type=MESH)
    greet(section > 0, {"tm": section - 1})
    greet(section < sections - 1, {"tm": section + 1})
    ends = [z > 0, z < lines - 1, section > 0, section < sections - 1]
    pl.semaphore_wait(barrier, 1 + sum(jnp.where(end, 1, 0) for end in ends))

    def blocks(arr, z0):
        return pieces if arr == 0 else (z0 * 2 * rows) // WIDE + 1

    def piece(arr, z0, y0, j):
        c = 2 * z0 + y0
        return factors.at[arr, pl.ds(pl.multiple_of(c * rows, rows), rows),
                          pl.ds(pl.multiple_of(j * WIDE, WIDE), WIDE)]

    def remote(way, arr, z0, y0, j):
        c = 2 * z0 + y0
        ref = piece(arr, z0, y0, j)
        to = {UP: col + 2, DOWN: col - 2, ACROSS: 2 * z + 1 - y}[way]
        return pltpu.make_async_remote_copy(
            src_ref=ref, dst_ref=ref, send_sem=send_sem.at[way, arr, c, j],
            recv_sem=recv_sem.at[arr, c, j], device_id={"cols": to}, device_id_type=MESH)

    def if_(cond, fn):
        pl.when(cond)(fn)

    def each(count, fn):
        def body(j, carry):
            fn(j)
            return carry
        lax.fori_loop(0, count, body, 0)

    def line(arr, act, received):
        def own_piece(j):
            if_(z < lines - 1, lambda: act(remote(UP, arr, z, y, j)))
            if_(z > 0, lambda: act(remote(DOWN, arr, z, y, j)))
            act(remote(ACROSS, arr, z, y, j))
        each(blocks(arr, z), own_piece)

        def hop(d, carry):
            def from_below(j):
                received(arr, z - d, y, j)
                if_(z < lines - 1, lambda: act(remote(UP, arr, z - d, y, j)))
                act(remote(ACROSS, arr, z - d, y, j))

            def from_above(j):
                received(arr, z + d, y, j)
                if_(z > 0, lambda: act(remote(DOWN, arr, z + d, y, j)))
                act(remote(ACROSS, arr, z + d, y, j))

            if_(z - d >= 0, lambda: each(blocks(arr, z - d), from_below))
            if_(z + d < lines, lambda: each(blocks(arr, z + d), from_above))
            return carry
        lax.fori_loop(1, lines, hop, 0)

    def received(arr, z0, y0, j):
        remote(ACROSS, arr, z0, y0, j).wait_recv()

    for arr in range(2):
        own[arr].wait()
        if arr == 0:
            loads[0].start()

            @pl.when(section == 0)
            def _():
                for copy in carries:
                    copy.start()
        line(arr, lambda copy: copy.start(), received)

    def across(arr):
        def from_line(z0, carry):
            each(blocks(arr, z0), lambda j: received(arr, z0, 1 - y, j))
            return carry
        lax.fori_loop(0, lines, from_line, 0)

    across(0)
    across(1)

    loads[0].wait()

    @pl.when(section == 0)
    def _():
        for copy in carries:
            copy.wait()

    def handed(b, i):
        span = pl.ds(i * WIDE, WIDE)
        return pltpu.make_async_remote_copy(
            src_ref=rounded.at[b, span, :], dst_ref=prior.at[b, span, :],
            send_sem=prior_send.at[b, i], recv_sem=prior_recv.at[b, i],
            device_id={"tm": section + 1}, device_id_type=MESH)

    def stored(b, i):
        span = pl.ds(i * WIDE, WIDE)
        return pltpu.make_async_copy(
            solved.at[b, span, :], out_ref.at[0, span, pl.ds(b * BATCH, BATCH)], store_sem.at[b, i])

    for b in range(batches):
        @pl.when(section > 0)
        def _():
            for i in range(pieces):
                handed(b, i).wait_recv()

        for i in range(pieces):
            span = pl.ds(i * WIDE, WIDE)
            coupled = jnp.dot(factors[0, span, :], prior[b], preferred_element_type=jnp.float32)
            source = rhs[span, pl.ds(b * BATCH, BATCH)].astype(jnp.float32)
            update[span, :] = (source - coupled).astype(jnp.bfloat16)
        for i in range(pieces):
            span = pl.ds(i * WIDE, WIDE)
            known = (i + 1) * WIDE
            result = jnp.dot(factors[1, span, :known], update[:known, :], preferred_element_type=jnp.float32)
            solved[b, span, :] = result
            rounded[b, span, :] = result.astype(jnp.bfloat16)
            stored(b, i).start()
            if_(section < sections - 1, lambda: handed(b, i).start())

    for arr in range(2):
        line(arr, lambda copy: copy.wait_send(), lambda *_: None)
    for b in range(batches):
        for i in range(pieces):
            stored(b, i).wait()
            if_(section < sections - 1, lambda: handed(b, i).wait_send())


def shards(sections, cols, inv_diag, sub_diag, rhs, carry_in):
    order, samples = carry_in.shape
    batches, pieces = samples // BATCH, order // WIDE
    flops = 4 * order * order * samples
    return pl.pallas_call(
        functools.partial(kernel, sections, cols // 2),
        out_shape=jax.ShapeDtypeStruct(rhs.shape, jnp.float32),
        in_specs=[pl.BlockSpec(memory_space=pl.ANY)] * 4,
        out_specs=pl.BlockSpec(memory_space=pl.ANY),
        scratch_shapes=[
            pltpu.VMEM((2, order, order), jnp.bfloat16),
            pltpu.VMEM((order, samples), jnp.bfloat16),
            pltpu.VMEM((batches, order, BATCH), jnp.bfloat16),
            pltpu.VMEM((order, BATCH), jnp.bfloat16),
            pltpu.VMEM((batches, order, BATCH), jnp.float32),
            pltpu.VMEM((batches, order, BATCH), jnp.bfloat16),
            pltpu.SemaphoreType.DMA((2,)),
            pltpu.SemaphoreType.DMA((1 + batches,)),
            pltpu.SemaphoreType.DMA((batches, pieces)),
            pltpu.SemaphoreType.DMA((3, 2, cols, pieces)),
            pltpu.SemaphoreType.DMA((2, cols, pieces)),
            pltpu.SemaphoreType.DMA((batches, pieces)),
            pltpu.SemaphoreType.DMA((batches, pieces)),
        ],
        compiler_params=pltpu.CompilerParams(
            collective_id=0, has_side_effects=True, vmem_limit_bytes=48 * 1024 * 1024),
        cost_estimate=pl.CostEstimate(flops=flops, bytes_accessed=10 * order * samples, transcendentals=0),
    )(inv_diag, sub_diag, rhs, carry_in)


def solution(mesh):
    in_specs = (
        P("tm", "cols", None),
        P("tm", "cols", None),
        P("tm", None, "cols"),
        P(None, "cols"),
    )
    out_specs = P("tm", None, "cols")
    body = functools.partial(shards, mesh.shape["tm"], mesh.shape["cols"])
    return jax.shard_map(body, mesh=mesh, in_specs=in_specs, out_specs=out_specs, check_vma=False)
```

time: 410 us -> 209 us (0.51)
  the two profiles are of different devices: /device:TPU:1 before, /device:TPU:3 now
where the time goes in v1:
time: 209 us
  Pallas kernels  200 us (96%)
  local copies, waits for them, and re-layouts  8.68 us (4%)
    pallas_call x1, Pallas kernels, shards(): pl.pallas_call(functools.partial(kernel, sections, cols // 2), out_shape=...  200 us
    unnamed x7, local copies, waits for them, and re-layouts  8.68 us

profile of v1, /device:TPU:3, one launch (start us, length us, event | category | flops | bytes accessed | tf_op | source)
XLA Modules:
  0.0 208.6 jit_solution(3814799265277783555)
XLA Ops:
  0.0 0.0 copy-start
  0.0 1.6 copy-done
  1.6 0.0 copy-start.1
  1.6 1.2 copy-done.1
  2.8 0.0 copy-start.2
  2.8 1.2 copy-done.2
  4.0 199.9 %shard_map.46 = f32[1,2048,512]{2,1,0:T(8,128)} custom-call(bf16[1,256,2048]{2,1,0:T(8,128)(2,1)S(1)} %copy-done.1, bf16[1,256,2048]{2,1,0:T(8,128)(2,1)S(1)} %copy-done.2, bf16[1,2048,512]{2,1,0:T(8,128)(2,1)S(1)} %copy-done, bf16[2048,512]{1,0:T(8,128)(2,1)} %carry_ref.1), custom_call_target="tpu_custom_call" | custom-call | flops 8589934592 | bytes 10485760 | tf_op jit(solution)/shard_map/pallas_call | solution.py:177
  204.0 4.6 %copy.6 = f32[1,2048,512]{2,1,0:T(8,128)} copy(f32[1,2048,512]{2,1,0:T(8,128)} %shard_map.46) | data formatting | bytes 8388608
Async XLA Ops:
  0.0 1.6 copy-start
  1.6 1.2 copy-start.1
  2.8 1.2 copy-start.2

commit v2 on v1

v2 whole, which is shorter than its diff:
```python
import functools

import jax
import jax.numpy as jnp
from jax import lax
from jax.experimental import pallas as pl
from jax.experimental.pallas import tpu as pltpu
from jax.sharding import PartitionSpec as P

MESH = pl.DeviceIdType.MESH
WIDE = 512
BATCH = 256
UP, DOWN, ACROSS = 0, 1, 2
TURN = 1


def kernel(sections, lines, inv_ref, sub_ref, rhs_ref, carry_ref, out_ref,
           factors, rhs, prior, update, solved, rounded,
           own_sem, load_sem, store_sem, send_sem, recv_sem, prior_send, prior_recv, turn_sem):
    section = lax.axis_index("tm")
    col = lax.axis_index("cols")
    z, y = col // 2, lax.rem(col, 2)
    rows = inv_ref.shape[1]
    order = inv_ref.shape[2]
    pieces = order // WIDE
    batches = rhs_ref.shape[2] // BATCH

    own_rows = pl.ds(pl.multiple_of(col * rows, rows), rows)
    own = [
        pltpu.make_async_copy(sub_ref.at[0], factors.at[0, own_rows, :], own_sem.at[0]),
        pltpu.make_async_copy(inv_ref.at[0], factors.at[1, own_rows, :], own_sem.at[1]),
    ]
    for copy in own:
        copy.start()
    loads = [pltpu.make_async_copy(rhs_ref.at[0], rhs, load_sem.at[0])]
    carries = [
        pltpu.make_async_copy(carry_ref.at[:, pl.ds(b * BATCH, BATCH)], prior.at[:, pl.ds(b * BATCH, BATCH)], load_sem.at[1 + b])
        for b in range(batches)
    ]

    barrier = pltpu.get_barrier_semaphore()

    def greet(cond, device):
        @pl.when(cond)
        def _():
            pl.semaphore_signal(barrier, inc=1, device_id=device, device_id_type=MESH)

    greet(z > 0, {"cols": col - 2})
    greet(z < lines - 1, {"cols": col + 2})
    pl.semaphore_signal(barrier, inc=1, device_id={"cols": 2 * z + 1 - y}, device_id_type=MESH)
    greet(section > 0, {"tm": section - 1})
    greet(section < sections - 1, {"tm": section + 1})
    ends = [z > 0, z < lines - 1, section > 0, section < sections - 1]
    pl.semaphore_wait(barrier, 1 + sum(jnp.where(end, 1, 0) for end in ends))

    def blocks(arr, z0):
        return pieces if arr == 0 else (z0 * 2 * rows) // WIDE + 1

    def piece(arr, z0, y0, j):
        c = 2 * z0 + y0
        return factors.at[arr, pl.ds(pl.multiple_of(c * rows, rows), rows),
                          pl.ds(pl.multiple_of(j * WIDE, WIDE), WIDE)]

    def remote(way, arr, z0, y0, j):
        c = 2 * z0 + y0
        ref = piece(arr, z0, y0, j)
        to = {UP: col + 2, DOWN: col - 2, ACROSS: 2 * z + 1 - y}[way]
        return pltpu.make_async_remote_copy(
            src_ref=ref, dst_ref=ref, send_sem=send_sem.at[way, arr, c, j],
            recv_sem=recv_sem.at[arr, c, j], device_id={"cols": to}, device_id_type=MESH)

    def if_(cond, fn):
        pl.when(cond)(fn)

    def each(count, fn):
        def body(j, carry):
            fn(j)
            return carry
        lax.fori_loop(0, count, body, 0)

    last = pieces - 1
    early = 2 * rows == WIDE and sections > 2

    def nth(arr, j):
        return lax.rem(j + last, pieces) if arr == 0 else j

    def along(arr, act, arrive, z0, y0, j, up, down):
        arrive(arr, z0, y0, j)
        if up:
            if_(z < lines - 1, lambda: act(remote(UP, arr, z0, y0, j)))
        if down:
            if_(z > 0, lambda: act(remote(DOWN, arr, z0, y0, j)))

    def line(arr, act, arrive, between=lambda d: None):
        def own_piece(k):
            j = nth(arr, k)
            act(remote(ACROSS, arr, z, y, j))
            along(arr, act, lambda *_: None, z, y, j, True, True)
        each(blocks(arr, z), own_piece)
        if arr == 0:
            along(arr, act, arrive, z, 1 - y, last, True, True)
        between(0)

        def from_side(z0, up):
            def one(k):
                j = nth(arr, k)
                along(arr, act, arrive, z0, y, j, up, not up)
                if arr == 0:
                    if_(j != last, lambda: act(remote(ACROSS, arr, z0, y, j)))
                else:
                    act(remote(ACROSS, arr, z0, y, j))
            each(blocks(arr, z0), one)
            if arr == 0:
                along(arr, act, arrive, z0, 1 - y, last, up, not up)

        def hop(d, carry):
            if_(z - d >= 0, lambda: from_side(z - d, True))
            if_(z + d < lines, lambda: from_side(z + d, False))
            return carry

        if early:
            for d in range(1, lines):
                hop(d, 0)
                between(d)
        else:
            lax.fori_loop(1, lines, hop, 0)

    def received(arr, z0, y0, j):
        remote(ACROSS, arr, z0, y0, j).wait_recv()

    def across(arr):
        def from_line(z0, carry):
            each(last if arr == 0 else blocks(arr, z0), lambda j: received(arr, z0, 1 - y, j))
            return carry
        lax.fori_loop(0, lines, from_line, 0)

    def handed(b, i):
        ref = (pl.ds(i * WIDE, WIDE), pl.ds(b * BATCH, BATCH))
        return pltpu.make_async_remote_copy(
            src_ref=rounded.at[ref], dst_ref=prior.at[ref],
            send_sem=prior_send.at[b, i], recv_sem=prior_recv.at[b, i],
            device_id={"tm": section + 1}, device_id_type=MESH)

    def stored(b, i):
        ref = (pl.ds(i * WIDE, WIDE), pl.ds(b * BATCH, BATCH))
        return pltpu.make_async_copy(solved.at[ref], out_ref.at[0].at[ref], store_sem.at[b, i])

    def couple(i, cols):
        span = pl.ds(i * WIDE, WIDE)
        coupled = jnp.dot(factors[0, span, :], prior[:, cols], preferred_element_type=jnp.float32)
        update[span, cols] = (rhs[span, cols].astype(jnp.float32) - coupled).astype(jnp.bfloat16)

    def solve(i, cols, parts):
        span = pl.ds(i * WIDE, WIDE)
        known = (i + 1) * WIDE
        result = jnp.dot(factors[1, span, :known], update[:known, cols], preferred_element_type=jnp.float32)
        rounded[span, cols] = result.astype(jnp.bfloat16)
        for b in parts:
            if_(section < sections - 1, lambda: handed(b, i).start())
        solved[span, cols] = result
        for b in parts:
            stored(b, i).start()

    whole = pl.ds(0, batches * BATCH)

    def solve_plane(z0):
        for i in range(pieces):
            @pl.when(z0 == i)
            def _():
                for j in range(i + 1):
                    received(1, i, 1 - y, j)
                solve(i, whole, range(batches))

    def between(d):
        @pl.when(section < 2)
        def _():
            if d == 0:
                @pl.when(section == 1)
                def _():
                    for b in range(batches):
                        for i in range(pieces):
                            handed(b, i).wait_recv()
                for i in range(pieces // 2):
                    couple(i, whole)
            elif d == 1:
                for i in range(pieces // 2, pieces):
                    couple(i, whole)
            elif d == 2:
                solve_plane(z)
            else:
                solve_plane(z - d + 2)
                solve_plane(z + d - 2)
        if d == TURN:
            @pl.when(section == 0)
            def _():
                pl.semaphore_signal(turn_sem, inc=1, device_id={"tm": section + 1}, device_id_type=MESH)

    own[0].wait()
    loads[0].start()

    @pl.when(section == 0)
    def _():
        for copy in carries:
            copy.start()
    if early:
        @pl.when(section == 1)
        def _():
            pl.semaphore_wait(turn_sem, 1)
    line(0, lambda copy: copy.start(), received)
    own[1].wait()
    loads[0].wait()

    @pl.when(section == 0)
    def _():
        for copy in carries:
            copy.wait()

    if early:
        def between_all(d):
            if d == 0:
                across(0)
            between(d)
        line(1, lambda copy: copy.start(), received, between_all)

        @pl.when(section < 2)
        def _():
            for d in (lines - 2, lines - 1):
                solve_plane(z - d)
                solve_plane(z + d)
    else:
        line(1, lambda copy: copy.start(), received)
        across(0)

    @pl.when(section >= (2 if early else 0))
    def _():
        across(1)
        for b in range(batches):
            @pl.when(section > 0)
            def _():
                for i in range(pieces):
                    handed(b, i).wait_recv()

            cols = pl.ds(b * BATCH, BATCH)
            for i in range(pieces):
                couple(i, cols)
            for i in range(pieces):
                solve(i, cols, (b,))

    for arr in range(2):
        line(arr, lambda copy: copy.wait_send(), lambda *_: None)
    for b in range(batches):
        for i in range(pieces):
            stored(b, i).wait()
            if_(section < sections - 1, lambda: handed(b, i).wait_send())


def shards(sections, cols, inv_diag, sub_diag, rhs, carry_in):
    order, samples = carry_in.shape
    batches, pieces = samples // BATCH, order // WIDE
    flops = 4 * order * order * samples
    return pl.pallas_call(
        functools.partial(kernel, sections, cols // 2),
        out_shape=jax.ShapeDtypeStruct(rhs.shape, jnp.float32),
        in_specs=[pl.BlockSpec(memory_space=pl.ANY)] * 4,
        out_specs=pl.BlockSpec(memory_space=pl.ANY),
        scratch_shapes=[
            pltpu.VMEM((2, order, order), jnp.bfloat16),
            pltpu.VMEM((order, samples), jnp.bfloat16),
            pltpu.VMEM((order, samples), jnp.bfloat16),
            pltpu.VMEM((order, samples), jnp.bfloat16),
            pltpu.VMEM((order, samples), jnp.float32),
            pltpu.VMEM((order, samples), jnp.bfloat16),
            pltpu.SemaphoreType.DMA((2,)),
            pltpu.SemaphoreType.DMA((1 + batches,)),
            pltpu.SemaphoreType.DMA((batches, pieces)),
            pltpu.SemaphoreType.DMA((3, 2, cols, pieces)),
            pltpu.SemaphoreType.DMA((2, cols, pieces)),
            pltpu.SemaphoreType.DMA((batches, pieces)),
            pltpu.SemaphoreType.DMA((batches, pieces)),
            pltpu.SemaphoreType.REGULAR,
        ],
        compiler_params=pltpu.CompilerParams(
            collective_id=0, has_side_effects=True, vmem_limit_bytes=48 * 1024 * 1024),
        cost_estimate=pl.CostEstimate(flops=flops, bytes_accessed=10 * order * samples, transcendentals=0),
    )(inv_diag, sub_diag, rhs, carry_in)


def solution(mesh):
    in_specs = (
        P("tm", "cols", None),
        P("tm", "cols", None),
        P("tm", None, "cols"),
        P(None, "cols"),
    )
    out_specs = P("tm", None, "cols")
    body = functools.partial(shards, mesh.shape["tm"], mesh.shape["cols"])
    return jax.shard_map(body, mesh=mesh, in_specs=in_specs, out_specs=out_specs, check_vma=False)
```

time: 209 us -> 192 us (0.919)
  Pallas kernels: 200 us -> 183 us
    pallas_call x1, Pallas kernels: 200 us -> 183 us  [shards(): pl.pallas_call(functools.partial(kernel, sections, cols // 2), out_shape=...]
where the time goes in v2:
time: 192 us; the launch traced here: 191 us
  Pallas kernels  183 us (95%)
  local copies, waits for them, and re-layouts  8.68 us (5%)
    pallas_call x1, Pallas kernels, shards(): pl.pallas_call(functools.partial(kernel, sections, cols // 2), out_shape=...  183 us
    unnamed x7, local copies, waits for them, and re-layouts  8.68 us

profile of v2, /device:TPU:3, one launch (start us, length us, event | category | flops | bytes accessed | tf_op | source)
XLA Modules:
  0.0 191.3 jit_solution(5371274938982121949)
XLA Ops:
  0.0 0.0 copy-start
  0.0 1.6 copy-done
  1.6 0.0 copy-start.1
  1.6 1.2 copy-done.1
  2.8 0.0 copy-start.2
  2.8 1.2 copy-done.2
  4.0 182.6 %shard_map.46 = f32[1,2048,512]{2,1,0:T(8,128)} custom-call(bf16[1,256,2048]{2,1,0:T(8,128)(2,1)S(1)} %copy-done.1, bf16[1,256,2048]{2,1,0:T(8,128)(2,1)S(1)} %copy-done.2, bf16[1,2048,512]{2,1,0:T(8,128)(2,1)S(1)} %copy-done, bf16[2048,512]{1,0:T(8,128)(2,1)} %carry_ref.1), custom_call_target="tpu_custom_call" | custom-call | flops 8589934592 | bytes 10485760 | tf_op jit(solution)/shard_map/pallas_call | solution.py:261
  186.6 4.6 %copy.6 = f32[1,2048,512]{2,1,0:T(8,128)} copy(f32[1,2048,512]{2,1,0:T(8,128)} %shard_map.46) | data formatting | bytes 8388608
Async XLA Ops:
  0.0 1.6 copy-start
  1.6 1.2 copy-start.1
  2.8 1.2 copy-start.2

commit v3 on v2

--- a/solution.py
+++ b/solution.py
@@ -11,7 +11,7 @@
 WIDE = 512
 BATCH = 256
 UP, DOWN, ACROSS = 0, 1, 2
-TURN = 1
+TURN = 0
 
 
 def kernel(sections, lines, inv_ref, sub_ref, rhs_ref, carry_ref, out_ref,
@@ -134,8 +134,11 @@
             return carry
         lax.fori_loop(0, lines, from_line, 0)
 
+    def rows_of(i):
+        return pl.ds(i * WIDE if isinstance(i, int) else pl.multiple_of(i * WIDE, WIDE), WIDE)
+
     def handed(b, i):
-        ref = (pl.ds(i * WIDE, WIDE), pl.ds(b * BATCH, BATCH))
+        ref = (rows_of(i), pl.ds(b * BATCH, BATCH))
         return pltpu.make_async_remote_copy(
             src_ref=rounded.at[ref], dst_ref=prior.at[ref],
             send_sem=prior_send.at[b, i], recv_sem=prior_recv.at[b, i],
@@ -234,17 +237,34 @@
     @pl.when(section >= (2 if early else 0))
     def _():
         across(1)
-        for b in range(batches):
+        solved[...] = rhs[...].astype(jnp.float32)
+
+        def add_group(g):
             @pl.when(section > 0)
             def _():
-                for i in range(pieces):
-                    handed(b, i).wait_recv()
-
-            cols = pl.ds(b * BATCH, BATCH)
+                for b in range(batches):
+                    handed(b, g).wait_recv()
+            group = pl.ds(pl.multiple_of(g * WIDE, WIDE), WIDE)
             for i in range(pieces):
-                couple(i, cols)
-            for i in range(pieces):
-                solve(i, cols, (b,))
+                span = pl.ds(i * WIDE, WIDE)
+                solved[span, :] -= jnp.dot(
+                    factors[0, span, group], prior[group, :], preferred_element_type=jnp.float32)
+
+        if early:
+            first = jnp.where(section == 2, z, 0)
+            add_group(first)
+
+            def next_groups(d, carry):
+                if_(first - d >= 0, lambda: add_group(first - d))
+                if_(first + d < lines, lambda: add_group(first + d))
+                return carry
+            lax.fori_loop(1, lines, next_groups, 0)
+        else:
+            lax.fori_loop(0, pieces, lambda g, carry: (add_group(g), carry)[1], 0)
+        for i in range(pieces):
+            span = pl.ds(i * WIDE, WIDE)
+            update[span, :] = solved[span, :].astype(jnp.bfloat16)
+            solve(i, whole, range(batches))
 
     for arr in range(2):
         line(arr, lambda copy: copy.wait_send(), lambda *_: None)

time: 192 us -> 186 us (0.969)
  Pallas kernels: 183 us -> 177 us
    pallas_call x1, Pallas kernels: 183 us -> 177 us  [shards(): pl.pallas_call(functools.partial(kernel, sections, cols // 2), out_shape=...]
where the time goes in v3:
time: 186 us
  Pallas kernels  177 us (95%)
  local copies, waits for them, and re-layouts  8.68 us (5%)
    pallas_call x1, Pallas kernels, shards(): pl.pallas_call(functools.partial(kernel, sections, cols // 2), out_shape=...  177 us
    unnamed x7, local copies, waits for them, and re-layouts  8.68 us

profile of v3, /device:TPU:3, one launch (start us, length us, event | category | flops | bytes accessed | tf_op | source)
XLA Modules:
  0.0 185.9 jit_solution(12300435100097564528)
XLA Ops:
  0.0 0.0 copy-start
  0.0 1.6 copy-done
  1.6 0.0 copy-start.1
  1.6 1.2 copy-done.1
  2.8 0.0 copy-start.2
  2.8 1.2 copy-done.2
  4.0 177.2 %shard_map.46 = f32[1,2048,512]{2,1,0:T(8,128)} custom-call(bf16[1,256,2048]{2,1,0:T(8,128)(2,1)S(1)} %copy-done.1, bf16[1,256,2048]{2,1,0:T(8,128)(2,1)S(1)} %copy-done.2, bf16[1,2048,512]{2,1,0:T(8,128)(2,1)S(1)} %copy-done, bf16[2048,512]{1,0:T(8,128)(2,1)} %carry_ref.1), custom_call_target="tpu_custom_call" | custom-call | flops 8589934592 | bytes 10485760 | tf_op jit(solution)/shard_map/pallas_call | solution.py:281
  181.3 4.6 %copy.6 = f32[1,2048,512]{2,1,0:T(8,128)} copy(f32[1,2048,512]{2,1,0:T(8,128)} %shard_map.46) | data formatting | bytes 8388608
Async XLA Ops:
  0.0 1.6 copy-start
  1.6 1.2 copy-start.1
  2.8 1.2 copy-start.2
